TPU v7x, 1024 devices: a whole 4x4x32 slice. The times are simulated.
1024 devices in a mesh: group: 32 (over z), fsdp: 32 (over y, x, core).
Axes of the slice: x: 4, y: 4, z: 32, core: 2. Of those that a mesh axis runs over, the one named last changes fastest.
Arguments:
- grad_blocks: bfloat16 [256, 1024, 1024], P('group', 'fsdp')
- stale_roots: bfloat16 [512, 1024, 1024], P('group', 'fsdp'), as said below
- fresh_roots: bfloat16 [512, 1024, 1024], P('group', 'fsdp'), as said below
- owner_list: int32 [32, 16], replicated, may hold values from 0 to 31, as said below
- slot_list: int32 [32, 16], replicated, may hold values from 0 to 15, as said below
- refresh_flags: int32 [32, 16], replicated, may hold values from 0 to 1
Outputs:
- updates: bfloat16 [256, 1024, 1024], P('group', 'fsdp')
Inputs may be any that keep to these rules, and one draw needn't show every extreme that they name: `stale_roots`: every block is symmetric. `fresh_roots`: every block is symmetric. `owner_list`: within one row the 16 owners are distinct. `slot_list`: two flagged entries with the same owner have different slots; the flagged entries of some owner use all 16 of its slots.
All inputs are finite; a program needn't handle non-finite values.
Results may differ from a plain program's by a relative error of at most 0.0049.
Values may be sent and summed in bfloat16 or wider, within the bound.
A program may use at most 32 MiB of HBM per device.

v0:
```python
import jax
import jax.numpy as jnp
from jax import lax
from jax.sharding import PartitionSpec as P

epsilon = 1e-06


def tile_return(
    scaled, exchanged_fn, shard_count, shard_pos, part_index, blocks, row_count, half_width
):
    row_half = part_index // 2
    group_span = shard_count // 2
    keep_half = (jnp.arange(2) == row_half)[:, None, None, None]
    outgoing_update = jnp.where(
        keep_half, scaled.reshape(1, group_span, row_count, half_width), jnp.bfloat16(0.0)
    )
    outgoing_update = outgoing_update.reshape(shard_count, row_count, half_width)
    returned = exchanged_fn(outgoing_update)
    returned = returned.reshape(blocks, 2, 2, row_count, half_width)
    chosen = jnp.take(returned, shard_pos // group_span, axis=1)
    return chosen.transpose(0, 2, 1, 3).reshape(blocks, row_count, 2 * half_width)


def local(grad_blocks, stale_roots, fresh_roots, owner_list, slot_list, refresh_flags):
    group_count = lax.axis_size("group")
    shard_count = lax.axis_size("fsdp")
    group_pos = lax.axis_index("group")
    shard_pos = lax.axis_index("fsdp")
    blocks, row_count, block_width = grad_blocks.shape
    roots_held = stale_roots.shape[0]
    half_width = block_width // 2
    flagged = refresh_flags == 1
    owned_here = jnp.logical_and(owner_list == group_pos, flagged)
    picked = jnp.sum(jnp.where(owned_here, slot_list, 0), axis=1)
    holding = jnp.any(owned_here, axis=1)
    selector = jnp.logical_and(
        picked[:, None] == jnp.arange(roots_held)[None, :], holding[:, None]
    ).astype(jnp.bfloat16)
    outgoing = jnp.einsum(
        "ts,sxw->txw", selector, fresh_roots, preferred_element_type=jnp.float32
    ).astype(jnp.bfloat16)
    arrived = lax.all_to_all(outgoing, "group", split_axis=0, concat_axis=0, tiled=True)
    own_owner = owner_list[group_pos]
    own_flag = flagged[group_pos]
    chooser = (own_owner[:, None] == jnp.arange(group_count)[None, :]).astype(jnp.bfloat16)
    delivered = jnp.einsum(
        "rt,txw->rxw", chooser, arrived, preferred_element_type=jnp.float32
    ).astype(jnp.bfloat16)
    current = jnp.where(own_flag[:, None, None], delivered, stale_roots)
    grad_square = jnp.sum(jnp.square(grad_blocks.astype(jnp.float32)), axis=(1, 2))
    spread = shard_count // blocks
    block_pos = shard_pos // spread
    part_index = shard_pos % spread
    left_roots = current[0::2]
    right_roots = current[1::2]
    contract_rows = (((0,), (0,)), ((), ()))
    tile_shape = (blocks, 2, 2, row_count, half_width)
    whole_grad = lax.all_to_all(
        jnp.repeat(grad_blocks, spread, axis=0), "fsdp", split_axis=0, concat_axis=1, tiled=True
    ).reshape(block_width, block_width)
    left_half = left_roots.reshape(blocks, row_count, 2, half_width).transpose(0, 2, 1, 3)
    right_half = right_roots.reshape(blocks, row_count, 2, half_width).transpose(0, 2, 1, 3)
    pieces = jnp.concatenate(
        [
            jnp.broadcast_to(left_half[:, :, None], tile_shape),
            jnp.broadcast_to(right_half[:, None], tile_shape),
        ],
        axis=4,
    ).reshape(shard_count, row_count, block_width)
    tiles_in = lax.all_to_all(pieces, "fsdp", split_axis=0, concat_axis=1, tiled=True).reshape(
        block_width, block_width
    )
    left_cols = tiles_in[:, :half_width]
    right_cols = tiles_in[:, half_width:]
    left_product = lax.dot_general(
        left_cols, whole_grad, contract_rows, preferred_element_type=jnp.float32
    ).astype(jnp.bfloat16)
    product = jnp.dot(left_product, right_cols, preferred_element_type=jnp.float32)
    own_block = jnp.arange(blocks) == block_pos
    update_square = jnp.where(own_block, jnp.sum(product * product), jnp.float32(0.0))
    grad_square, update_square = lax.psum((grad_square, update_square), "fsdp")
    graft_ratio = jnp.sqrt(grad_square) * lax.rsqrt(update_square + epsilon)
    scaled = (graft_ratio[block_pos] * product).astype(jnp.bfloat16)

    def send_tiles(outgoing_update):
        return lax.all_to_all(outgoing_update, "fsdp", split_axis=0, concat_axis=0, tiled=True)

    return tile_return(
        scaled, send_tiles, shard_count, shard_pos, part_index, blocks, row_count, half_width
    )


def solution(mesh):
    placed = (
        P("group", "fsdp", None),
        P("group", "fsdp", None),
        P("group", "fsdp", None),
        P(),
        P(),
        P(),
    )
    return jax.shard_map(
        local, mesh=mesh, in_specs=placed, out_specs=P("group", "fsdp", None), check_vma=False
    )
```

profile of v0, /device:TPU:1, one launch (start us, length us, event | category | flops | bytes accessed | tf_op | source)
XLA Modules:
  0.0 396.4 jit_solution(3314792828235459245)
XLA Ops:
  0.0 0.0 copy-start
  0.0 0.8 fusion.22
  0.8 0.7 select_reduce_fusion
  1.5 0.0 copy-done
  1.5 0.9 convolution_convert_fusion
  2.4 1.2 copy.19
  3.6 0.0 copy-start.1
  3.6 224.3 %all_to_all.28 = bf16[32,32,1024]{2,1,0:T(8,128)(2,1)} all-to-all(bf16[32,32,1024]{2,1,0:T(8,128)(2,1)S(1)} %copy.19), channel_id=1, replica_groups=mesh['group'=32,'fsdp'=32] {'group'}, dimensions={0} | all-to-all | bytes 4194304 | tf_op jit(solution)/shard_map/all_to_all | solution.py:43
  227.9 0.0 copy-done.1
  227.9 1.6 broadcast_in_dim.92
  229.4 0.0 copy-start.2
  229.4 0.0 copy-start.3
  229.4 8.3 %all-to-all-start.2 = ((bf16[32,32,1024]{2,1,0:T(8,128)(2,1)}), bf16[32,32,1024]{2,1,0:T(8,128)(2,1)}, u32[]{:S(2)}, u32[]{:S(2)}) async-start(bf16[32,32,1024]{2,1,0:T(8,128)(2,1)} %bitcast.8), calls=%async_computation.2 | async-start | bytes 4194304 | tf_op jit(solution)/shard_map/all_to_all | solution.py:59
  237.8 0.0 copy-done.2
  237.8 0.2 dynamic-slice_reduce_fusion
  238.0 0.2 dynamic-slice_reduce_fusion.1
  238.2 0.0 copy-done.3
  238.2 5.7 %fusion.5 = bf16[16,32,1024]{2,0,1:T(8,128)(2,1)} fusion(bf16[32,32,1024]{2,1,0:T(8,128)(2,1)} %all_to_all.28, bf16[16,32,1024]{2,1,0:T(8,128)(2,1)S(1)} %copy-done.3, pred[16]{0:T(512)(128)(4,1)S(1)} %dynamic-slice_reduce_fusion.1, s32[16]{0:T(128)S(1)} %dynamic-slice_reduce_fusion), kind=kOutput, calls=%fused_computation.6 | convolution fusion | flops 34603520 | bytes 4194384 | tf_op jit(solution)/shard_map/rt,txw->rxw/dot_general | solution.py:47
  243.9 4.0 slice.13
  247.9 4.0 %slice.12 = bf16[8,32,1024]{2,0,1:T(8,128)(2,1)S(1)} slice(bf16[16,32,1024]{2,0,1:T(8,128)(2,1)} %fusion.5), slice={[0:16:2], [0:32:1], [0:1024:1]} | slice | bytes 1048576 | tf_op jit(solution)/shard_map/slice | solution.py:55
  251.8 0.3 copy.23
  252.1 0.3 copy.22
  252.4 0.1 broadcast_in_dim.91
  252.6 0.1 broadcast_in_dim.90
  252.7 1.6 pad_maximum_fusion
  254.3 11.4 %all-to-all-done.2 = bf16[32,32,1024]{2,1,0:T(8,128)(2,1)} async-done(((bf16[32,32,1024]{2,1,0:T(8,128)(2,1)}), bf16[32,32,1024]{2,1,0:T(8,128)(2,1)}, u32[]{:S(2)}, u32[]{:S(2)}) %all-to-all-start.2) | async-done | bytes 2097184 | tf_op jit(solution)/shard_map/all_to_all | solution.py:59
  265.7 6.7 %all-to-all-start.1 = ((bf16[32,32,1024]{2,1,0:T(8,128)(2,1)}), bf16[32,32,1024]{2,1,0:T(8,128)(2,1)}, u32[]{:S(2)}, u32[]{:S(2)}) async-start(bf16[32,32,1024]{2,1,0:T(8,128)(2,1)} %bitcast.6), calls=%async_computation.1 | async-start | bytes 4194304 | tf_op jit(solution)/shard_map/all_to_all | solution.py:71
  272.5 0.1 broadcast_in_dim.84
  272.5 0.1 broadcast_in_dim.85
  272.6 0.2 multiply_reduce_fusion.1
  272.8 27.6 %all-to-all-done.1 = bf16[32,32,1024]{2,1,0:T(8,128)(2,1)} async-done(((bf16[32,32,1024]{2,1,0:T(8,128)(2,1)}), bf16[32,32,1024]{2,1,0:T(8,128)(2,1)}, u32[]{:S(2)}, u32[]{:S(2)}) %all-to-all-start.1) | async-done | bytes 2097184 | tf_op jit(solution)/shard_map/all_to_all | solution.py:71
  300.4 4.7 %multiply_reduce_fusion = (f32[]{:T(128)}, f32[512,512]{1,0:T(8,128)S(1)}) fusion(bf16[1024,1024]{1,0:T(8,128)(2,1)} %bitcast.7, bf16[1024,1024]{1,0:T(8,128)(2,1)} %bitcast.9), kind=kOutput, calls=%fused_computation.13 | convolution fusion | flops 1611661312 | bytes 5242884 | tf_op jit(solution)/shard_map/dot_general | solution.py:79
  305.1 0.6 compare_select_fusion
  305.8 64.4 %all-reduce = (f32[8]{0:T(128)S(1)}, f32[8]{0:T(128)S(1)}) all-reduce(f32[8]{0:T(128)S(1)} %compare_select_fusion, f32[8]{0:T(128)S(1)} %multiply_reduce_fusion.1), channel_id=1, replica_groups=mesh['group'=32,'fsdp'=32] {'fsdp'}, use_global_device_ids=true, to_apply=%region_5.6 | all-reduce | flops 16 | bytes 128 | tf_op jit(solution)/shard_map/psum | solution.py:82
  370.2 0.6 dynamic_slice.11
  370.8 0.8 multiply_convert_fusion
  371.6 1.1 bitcast_select_fusion
  372.7 5.4 %all-to-all-start.3 = ((bf16[32,32,512]{2,1,0:T(8,128)(2,1)}), bf16[32,32,512]{2,1,0:T(8,128)(2,1)S(1)}, u32[]{:S(2)}, u32[]{:S(2)}) async-start(bf16[32,32,512]{2,1,0:T(8,128)(2,1)} %bitcast_select_fusion), calls=%async_computation.3 | async-start | bytes 2097152 | tf_op jit(solution)/shard_map/all_to_all | solution.py:87
  378.2 17.3 %all-to-all-done.3 = bf16[32,32,512]{2,1,0:T(8,128)(2,1)S(1)} async-done(((bf16[32,32,512]{2,1,0:T(8,128)(2,1)}), bf16[32,32,512]{2,1,0:T(8,128)(2,1)S(1)}, u32[]{:S(2)}, u32[]{:S(2)}) %all-to-all-start.3) | async-done | bytes 1048608 | tf_op jit(solution)/shard_map/all_to_all | solution.py:87
  395.5 0.1 select_bitcast_fusion
  395.5 0.9 copy.25
  (2 shorter events, 0.0 us)
Async XLA Ops:
  0.0 1.5 copy-start
  3.6 224.3 %copy-start.1 = (bf16[8,32,1024]{2,1,0:T(8,128)(2,1)S(1)}, bf16[8,32,1024]{2,1,0:T(8,128)(2,1)}, u32[]{:S(2)}) copy-start(bf16[8,32,1024]{2,1,0:T(8,128)(2,1)} %param.6) | copy-start | bytes 1572868
  229.4 8.4 %copy-start.2 = (s32[32,16]{0,1:T(8,128)S(1)}, s32[32,16]{0,1:T(8,128)}, u32[]{:S(2)}) copy-start(s32[32,16]{0,1:T(8,128)} %param.9) | copy-start | bytes 6148
  229.4 8.7 %copy-start.3 = (bf16[16,32,1024]{2,1,0:T(8,128)(2,1)S(1)}, bf16[16,32,1024]{2,1,0:T(8,128)(2,1)}, u32[]{:S(2)}) copy-start(bf16[16,32,1024]{2,1,0:T(8,128)(2,1)} %param.7) | copy-start | bytes 3145732
  229.4 36.2 %all-to-all-start.2 = ((bf16[32,32,1024]{2,1,0:T(8,128)(2,1)}), bf16[32,32,1024]{2,1,0:T(8,128)(2,1)}, u32[]{:S(2)}, u32[]{:S(2)}) async-start(bf16[32,32,1024]{2,1,0:T(8,128)(2,1)} %bitcast.8), calls=%async_computation.2 | async-start | bytes 4194304 | tf_op jit(solution)/shard_map/all_to_all | solution.py:59
  265.7 34.7 %all-to-all-start.1 = ((bf16[32,32,1024]{2,1,0:T(8,128)(2,1)}), bf16[32,32,1024]{2,1,0:T(8,128)(2,1)}, u32[]{:S(2)}, u32[]{:S(2)}) async-start(bf16[32,32,1024]{2,1,0:T(8,128)(2,1)} %bitcast.6), calls=%async_computation.1 | async-start | bytes 4194304 | tf_op jit(solution)/shard_map/all_to_all | solution.py:71
  372.7 22.7 %all-to-all-start.3 = ((bf16[32,32,512]{2,1,0:T(8,128)(2,1)}), bf16[32,32,512]{2,1,0:T(8,128)(2,1)S(1)}, u32[]{:S(2)}, u32[]{:S(2)}) async-start(bf16[32,32,512]{2,1,0:T(8,128)(2,1)} %bitcast_select_fusion), calls=%async_computation.3 | async-start | bytes 2097152 | tf_op jit(solution)/shard_map/all_to_all | solution.py:87
where the time goes:
time: 397 us; the launch traced here: 396 us
  blocking collectives  289 us (73%)
  waiting for transfers between devices  56.2 us (14%)
  starting transfers between devices  20.5 us (5%)
  local copies, waits for them, and re-layouts  13.5 us (3%)
  matrix products  11.3 us (3%)
  other arithmetic  5.98 us (2%)
    all_to_all x1, blocking collectives, local(): lax.all_to_all(outgoing, 'group', split_axis=0, concat_axis=0, tiled=True)  224 us
    psum x1, blocking collectives, local(): grad_square, update_square = lax.psum((grad_square, update_square), 'fsdp')  64.4 us
    all_to_all x1, waiting for transfers between devices, local(): lax.all_to_all(pieces, 'fsdp', split_axis=0, concat_axis=1, tiled=True)  27.6 us
    all_to_all x1, waiting for transfers between devices, send_tiles(): lax.all_to_all(outgoing_update, 'fsdp', split_axis=0, concat_axis=0, tile...  17.3 us
    all_to_all x1, waiting for transfers between devices, local(): lax.all_to_all(jnp.repeat(grad_blocks, spread, axis=0), 'fsdp', split_axi...  11.4 us
    all_to_all x1, starting transfers between devices, local(): lax.all_to_all(jnp.repeat(grad_blocks, spread, axis=0), 'fsdp', split_axi...  8.35 us
  transfers between devices with their start and end apart: 3, of which 3 were waited for; matrix products, arithmetic and copies ran while one was open for 4% of the time, Pallas kernels for 0%

commit v1 on v0

--- a/solution.py
+++ b/solution.py
@@ -1,9 +1,32 @@
+import functools
+
 import jax
 import jax.numpy as jnp
 from jax import lax
+from jax.experimental import pallas as pl
+from jax.experimental.pallas import tpu as pltpu
 from jax.sharding import PartitionSpec as P
 
 epsilon = 1e-06
+MESH = pl.DeviceIdType.MESH
+GROUPS = 32
+SHARDS = 32
+ROOTS = 16
+BLOCKS = 8
+ROWS = 32
+WIDTH = 1024
+HALF = 512
+TILE = 128
+SUPER = 8
+BAND = 640
+REST = 384
+REACH = 16
+HOPS = 18
+TRAINS = 4
+STEPS = HOPS * TRAINS
+DIST_ROWS = 2 * STEPS
+OK_ROW = DIST_ROWS + 2 * REACH
+TABLE_ROWS = OK_ROW + 8
 
 
 def tile_return(
@@ -22,7 +45,7 @@
     return chosen.transpose(0, 2, 1, 3).reshape(blocks, row_count, 2 * half_width)
 
 
-def local(grad_blocks, stale_roots, fresh_roots, owner_list, slot_list, refresh_flags):
+def whole_exchange(grad_blocks, stale_roots, fresh_roots, owner_list, slot_list, refresh_flags):
     group_count = lax.axis_size("group")
     shard_count = lax.axis_size("fsdp")
     group_pos = lax.axis_index("group")
@@ -91,6 +114,463 @@
     )
 
 
+def schedule_kernel(packed_ref, table_ref, ahead, log):
+    group_pos = lax.axis_index("group")
+    lane = lax.broadcasted_iota(jnp.int32, (1, TILE), 1)
+    node = lane % GROUPS
+    rows = lax.broadcasted_iota(jnp.int32, (REACH, TILE), 0)
+    packed = packed_ref[...]
+    owner = jnp.where(packed < 0, -1, packed // 32)
+    value = jnp.where(packed < 0, 0, packed % 32 + 1)
+    for dist in range(1, GROUPS):
+        shift = (TILE - dist) % TILE
+        match = pltpu.roll(owner, shift, 1) == node
+        line = jnp.max(jnp.where(match, pltpu.roll(value, shift, 1), 0), axis=0, keepdims=True)
+        if dist <= REACH:
+            near = jnp.where(line > 0, line + dist * 32, 0)
+            if dist == REACH:
+                near = jnp.where(node % 2 == 0, near, 0)
+            ahead[0, dist - 1 : dist, :] = near
+        if dist >= REACH:
+            back = GROUPS - dist
+            near = jnp.where(line > 0, line + back * 32, 0)
+            if dist == REACH:
+                near = jnp.where(node % 2 == 1, near, 0)
+            ahead[1, back - 1 : back, :] = near
+
+    def hop(index, carry):
+        waiting, arrived, remain, whole = carry
+        waiting, arrived = list(waiting), list(arrived)
+        remain, whole = list(remain), list(whole)
+        for train in range(TRAINS):
+            place = index * TRAINS + train
+            for way in range(2):
+                at = train * 2 + way
+                best = jnp.max(waiting[way], axis=0, keepdims=True)
+                taken = jnp.logical_and(remain[at] == 0, best > 0)
+                code = jnp.where(taken, best, 0)
+                waiting[way] = jnp.where(waiting[way] == jnp.where(taken, best, -1), 0, waiting[way])
+                log[pl.ds(way * STEPS + place, 1), :] = code % 32 - 1
+                dist = code // 32
+                left = jnp.where(taken, dist, remain[at])
+                total = jnp.where(taken, dist, whole[at])
+                shift = 1 if way == 0 else TILE - 1
+                left = pltpu.roll(jnp.maximum(left - 1, 0), shift, 1)
+                total = pltpu.roll(total, shift, 1)
+                done = jnp.where(left == 0, total, 0)
+                arrived[way] = jnp.where(rows + 1 == done, place, arrived[way])
+                remain[at] = left
+                whole[at] = jnp.where(left == 0, 0, total)
+        return tuple(waiting), tuple(arrived), tuple(remain), tuple(whole)
+
+    zero = jnp.zeros((1, TILE), jnp.int32)
+    none = jnp.zeros((REACH, TILE), jnp.int32)
+    start = (
+        (ahead[0], ahead[1]),
+        (none, none),
+        (zero,) * (2 * TRAINS),
+        (zero,) * (2 * TRAINS),
+    )
+    waiting, arrived, remain, _ = lax.fori_loop(0, HOPS, hop, start)
+    log[DIST_ROWS : DIST_ROWS + REACH, :] = arrived[0]
+    log[DIST_ROWS + REACH : OK_ROW, :] = arrived[1]
+    open_count = jnp.max(jnp.maximum(waiting[0], waiting[1]), axis=0, keepdims=True)
+    for count in remain:
+        open_count = jnp.maximum(open_count, count)
+    open_count = jnp.max(open_count, axis=1, keepdims=True)
+    log[OK_ROW:TABLE_ROWS, :] = jnp.broadcast_to(open_count, (8, TILE))
+    own = jnp.sum(jnp.where(lane == group_pos, log[...], 0), axis=1, keepdims=True)
+    table_ref[...] = jnp.broadcast_to(own, (TABLE_ROWS, TILE))
+
+
+def schedule(packed):
+    lanes = jnp.tile(packed.T, (1, TILE // GROUPS))
+    table = pl.pallas_call(
+        schedule_kernel,
+        out_shape=jax.ShapeDtypeStruct((TABLE_ROWS, TILE), jnp.int32),
+        in_specs=[pl.BlockSpec(memory_space=pltpu.VMEM)],
+        out_specs=pl.BlockSpec(memory_space=pltpu.VMEM),
+        scratch_shapes=[
+            pltpu.VMEM((2, REACH, TILE), jnp.int32),
+            pltpu.VMEM((TABLE_ROWS, TILE), jnp.int32),
+        ],
+    )(lanes)
+    return table[:, 0]
+
+
+def turned(tile):
+    return tile.astype(jnp.float32).T.astype(jnp.bfloat16)
+
+
+def fill(inner, outer):
+    for row in range(4):
+        for col in range(row):
+            inner[row * TILE : (row + 1) * TILE, col * TILE : (col + 1) * TILE] = turned(
+                inner[col * TILE : (col + 1) * TILE, row * TILE : (row + 1) * TILE]
+            )
+        for col in range(row + 5, SUPER):
+            away = row + SUPER - col - 1
+            inner[row * TILE : (row + 1) * TILE, col * TILE : (col + 1) * TILE] = turned(
+                outer[(col - 4) * TILE : (col - 3) * TILE, away * TILE : (away + 1) * TILE]
+            )
+
+
+def main_kernel(
+    table, packed, grad, stale, fresh, out,
+    fresh_band, stale_band, current, sending, log, whole_grad,
+    left_in, left_out, right_in, right_out, left_product, product, tile, sums, sums_out,
+    load_sem, ring_send, ring_recv, grad_send, grad_recv, left_send, left_recv,
+    right_send, right_recv, sum_send, sum_recv, own_sem, tile_send, tile_recv,
+):
+    z = lax.axis_index("group")
+    f = lax.axis_index("fsdp")
+    onward = (lax.rem(z + 1, GROUPS), lax.rem(z + GROUPS - 1, GROUPS))
+    superblock = f // 4
+    block = f // 4
+    part = lax.rem(f, 4)
+    row_half = part // 2
+    col_half = lax.rem(part, 2)
+
+    loads = []
+    for number, (source, target) in enumerate(((fresh, fresh_band), (stale, stale_band))):
+        for col in range(5):
+            start = pl.multiple_of(lax.rem(superblock + col, SUPER) * TILE, TILE)
+            load = pltpu.make_async_copy(
+                source.at[:, :, pl.ds(start, TILE)],
+                target.at[:, :, pl.ds(col * TILE, TILE)],
+                load_sem.at[number, col],
+            )
+            load.start()
+            loads.append(load)
+
+    barrier = pltpu.get_barrier_semaphore()
+    for peer in onward:
+        pl.semaphore_signal(barrier, inc=1, device_id=(peer, f), device_id_type=MESH)
+
+    def greet(step, carry):
+        peer = lax.rem(f + step, SHARDS)
+        pl.semaphore_signal(barrier, inc=1, device_id=(z, peer), device_id_type=MESH)
+        return carry
+
+    lax.fori_loop(1, SHARDS, greet, 0)
+    for load in loads:
+        load.wait()
+    pl.semaphore_wait(barrier, SHARDS + 1)
+
+    def grad_copy(peer):
+        row = lax.rem(f + SHARDS - 16 * (lax.rem(peer, 4) // 2), SHARDS)
+        return (
+            grad.at[peer // 4],
+            whole_grad.at[pl.ds(pl.multiple_of(row * ROWS, ROWS), ROWS), :],
+        )
+
+    def grad_remote(peer):
+        source, target = grad_copy(peer)
+        return pltpu.make_async_remote_copy(
+            src_ref=source, dst_ref=target, send_sem=grad_send.at[peer], recv_sem=grad_recv,
+            device_id=(z, peer), device_id_type=MESH,
+        )
+
+    def each_peer(act):
+        lax.fori_loop(1, SHARDS, lambda s, c: (act(lax.rem(f + s, SHARDS)), c)[1], 0)
+
+    def ring_copy(way, index, train):
+        turn = lax.rem(index, 3)
+        return pltpu.make_async_remote_copy(
+            src_ref=sending.at[(way * 3 + turn) * TRAINS + train],
+            dst_ref=log.at[way * STEPS + index * TRAINS + train],
+            send_sem=ring_send.at[way, turn, train],
+            recv_sem=ring_recv.at[way, index, train],
+            device_id=(onward[way], f),
+            device_id_type=MESH,
+        )
+
+    def hop(index, first):
+        for train in range(TRAINS):
+            for way in range(2):
+                place = index * TRAINS + train
+                choice = table[way * STEPS + place]
+                own = fresh_band[jnp.maximum(choice, 0)]
+                turn = lax.rem(index, 3)
+                if not first:
+                    ring_copy(way, index - 1, train).wait_recv()
+
+                    @pl.when(index >= 3)
+                    def _():
+                        ring_copy(way, index - 3, train).wait_send()
+
+                    own = jnp.where(choice < 0, log[way * STEPS + place - TRAINS], own)
+                sending[(way * 3 + turn) * TRAINS + train] = own
+                ring_copy(way, index, train).start()
+
+    hop(0, True)
+    each_peer(lambda peer: grad_remote(peer).start())
+    own_grad = pltpu.make_async_copy(*grad_copy(f), grad_recv)
+    own_grad.start()
+    lax.fori_loop(1, HOPS, lambda i, c: (hop(i, False), c)[1], 0)
+
+    pltpu.make_async_copy(whole_grad, whole_grad, grad_recv).wait()
+
+    def add_squares(index, total):
+        rows = whole_grad[pl.ds(pl.multiple_of(index * 32, 32), 32), :].astype(jnp.float32)
+        squares = (rows * rows).reshape(4, 8, 8, TILE)
+        return total + jnp.sum(squares, axis=(0, 2))
+
+    grad_square = lax.fori_loop(0, WIDTH // 32, add_squares, jnp.zeros((8, TILE), jnp.float32))
+
+    for way in range(2):
+        for train in range(TRAINS):
+            ring_copy(way, HOPS - 1, train).wait_recv()
+            for turn in range(3):
+                ring_copy(way, HOPS - 3 + turn, train).wait_send()
+
+    for root in range(ROOTS):
+        code = packed[z * ROOTS + root]
+        used = jnp.maximum(code, 0)
+        owner = used // 32
+        slot = lax.rem(used, 32)
+        away = lax.rem(z - owner + GROUPS, GROUPS)
+        ahead = jnp.logical_or(away < REACH, jnp.logical_and(away == REACH, lax.rem(owner, 2) == 0))
+        dist = jnp.where(ahead, away, GROUPS - away)
+        way = jnp.where(ahead, 0, 1)
+        found = table[DIST_ROWS + way * REACH + jnp.maximum(dist - 1, 0)]
+        moved = log[way * STEPS + found]
+        own = jnp.where(away == 0, fresh_band[slot], moved)
+        current[root] = jnp.where(code < 0, stale_band[root], own)
+
+    def root_copies(number, half, peer_half, peer, inner, outer, send, recv, recv_out):
+        place = lax.rem(f + SHARDS - 16 * peer_half, SHARDS)
+        first_row = pl.multiple_of(lax.rem(place, 16) * ROWS, ROWS)
+        col = pl.multiple_of(lax.rem(place // 4, 4) * TILE, TILE)
+        near = (
+            current.at[number],
+            inner.at[pl.ds(first_row, ROWS), pl.ds(col, BAND)],
+        )
+        far = (
+            current.at[number, :, pl.ds(TILE, REST)],
+            outer.at[pl.ds(first_row, ROWS), :],
+        )
+        return place < 16, near, far
+
+    def root_send(side, peer, wait):
+        part = lax.rem(peer, 4)
+        half = part // 2 if side == 0 else lax.rem(part, 2)
+        number = (peer // 4) * 2 + side
+        inner, outer, send, recv = (
+            (left_in, left_out, left_send, left_recv),
+            (right_in, right_out, right_send, right_recv),
+        )[side]
+        is_near, near, far = root_copies(number, 0, half, peer, inner, outer, send, recv, recv)
+
+        def go(pair, sem):
+            copy = pltpu.make_async_remote_copy(
+                src_ref=pair[0], dst_ref=pair[1], send_sem=send.at[peer], recv_sem=sem,
+                device_id=(z, peer), device_id_type=MESH,
+            )
+            if wait:
+                copy.wait_send()
+            else:
+                copy.start()
+
+        @pl.when(is_near)
+        def _():
+            go(near, recv.at[0])
+
+        @pl.when(jnp.logical_not(is_near))
+        def _():
+            go(far, recv.at[1])
+
+    def root_own(side):
+        part = lax.rem(f, 4)
+        half = part // 2 if side == 0 else lax.rem(part, 2)
+        number = (f // 4) * 2 + side
+        inner, outer, recv = ((left_in, left_out, left_recv), (right_in, right_out, right_recv))[side]
+        is_near, near, far = root_copies(number, 0, half, f, inner, outer, None, None, None)
+
+        @pl.when(is_near)
+        def _():
+            pltpu.make_async_copy(*near, recv.at[0]).start()
+
+        @pl.when(jnp.logical_not(is_near))
+        def _():
+            pltpu.make_async_copy(*far, recv.at[1]).start()
+
+    def root_wait(side):
+        inner, outer, recv = ((left_in, left_out, left_recv), (right_in, right_out, right_recv))[side]
+        window = inner.at[:, pl.ds(0, BAND)]
+        pltpu.make_async_copy(window, window, recv.at[0]).wait()
+        pltpu.make_async_copy(outer, outer, recv.at[1]).wait()
+
+    for side in range(2):
+        each_peer(functools.partial(root_send, side, wait=False))
+        root_own(side)
+
+    root_wait(0)
+    fill(left_in, left_out)
+    first_rows = pl.ds(0, HALF)
+
+    def left_step(index, carry):
+        cols = pl.ds(pl.multiple_of(index * 256, 256), 256)
+        left_product[:, cols] = jnp.dot(
+            left_in[...], whole_grad[:, cols], preferred_element_type=jnp.float32
+        ).astype(jnp.bfloat16)
+        return carry
+
+    lax.fori_loop(0, 4, left_step, 0)
+    root_wait(1)
+    fill(right_in, right_out)
+    near_cols = pl.ds(pl.multiple_of(col_half * HALF, HALF), HALF)
+    far_cols = pl.ds(pl.multiple_of((1 - col_half) * HALF, HALF), HALF)
+    contract_last = (((1,), (1,)), ((), ()))
+
+    def right_step(index, total):
+        rows = pl.ds(pl.multiple_of(index * TILE, TILE), TILE)
+        value = lax.dot_general(
+            left_product[rows, near_cols], right_in[:, :HALF], contract_last,
+            preferred_element_type=jnp.float32,
+        ) + lax.dot_general(
+            left_product[rows, far_cols], right_in[:, HALF:], contract_last,
+            preferred_element_type=jnp.float32,
+        )
+        product[rows, :] = value
+        squares = (value * value).reshape(16, 8, 4, TILE)
+        return total + jnp.sum(squares, axis=(0, 2))
+
+    own_square = lax.fori_loop(0, 4, right_step, jnp.zeros((8, TILE), jnp.float32))
+    sums_out[...] = own_square
+
+    def sum_copy(step):
+        peer = (f // 4) * 4 + lax.rem(part + step, 4)
+        return pltpu.make_async_remote_copy(
+            src_ref=sums_out, dst_ref=sums.at[part], send_sem=sum_send.at[step - 1],
+            recv_sem=sum_recv, device_id=(z, peer), device_id_type=MESH,
+        )
+
+    for step in range(1, 4):
+        sum_copy(step).start()
+    pltpu.make_async_copy(sums_out, sums.at[part], sum_recv).start()
+    pltpu.make_async_copy(sums, sums, sum_recv).wait()
+    update_square = (sums[0] + sums[1]) + (sums[2] + sums[3])
+    update_square = jnp.sum(update_square, axis=(0, 1), keepdims=True)
+    grad_total = jnp.sum(grad_square, axis=(0, 1), keepdims=True)
+    ratio = jnp.sqrt(grad_total) * lax.rsqrt(update_square + epsilon)
+
+    def scale_step(index, carry):
+        rows = pl.ds(pl.multiple_of(index * 64, 64), 64)
+        tile[rows, :] = (ratio * product[rows, :]).astype(jnp.bfloat16)
+        return carry
+
+    lax.fori_loop(0, 8, scale_step, 0)
+
+    def tile_copy(step):
+        row = pl.multiple_of(step * ROWS, ROWS)
+        return (
+            tile.at[pl.ds(row, ROWS), :],
+            out.at[block, :, pl.ds(pl.multiple_of(col_half * HALF, HALF), HALF)],
+        )
+
+    def tile_remote(step):
+        source, target = tile_copy(step)
+        return pltpu.make_async_remote_copy(
+            src_ref=source, dst_ref=target, send_sem=tile_send.at[step], recv_sem=tile_recv,
+            device_id=(z, row_half * 16 + step), device_id_type=MESH,
+        )
+
+    def tile_act(wait):
+        def act(step, carry):
+            turn = lax.rem(f + step, 16)
+
+            @pl.when(row_half * 16 + turn != f)
+            def _():
+                copy = tile_remote(turn)
+                if wait:
+                    copy.wait_send()
+                else:
+                    copy.start()
+
+            return carry
+
+        lax.fori_loop(0, 16, act, 0)
+
+    tile_act(False)
+
+    @pl.when(row_half == f // 16)
+    def _():
+        pltpu.make_async_copy(*tile_copy(lax.rem(f, 16)), tile_recv).start()
+
+    each_peer(lambda peer: grad_remote(peer).wait_send())
+    for side in range(2):
+        each_peer(functools.partial(root_send, side, wait=True))
+    for step in range(1, 4):
+        sum_copy(step).wait_send()
+    tile_act(True)
+    pltpu.make_async_copy(out, out, tile_recv).wait()
+
+
+def ring_exchange(table, packed, grad_blocks, stale_roots, fresh_roots):
+    bf16, f32 = jnp.bfloat16, jnp.float32
+    dma = pltpu.SemaphoreType.DMA
+    vmem = pltpu.VMEM
+    smem_spec = pl.BlockSpec(memory_space=pltpu.SMEM)
+    any_spec = pl.BlockSpec(memory_space=pl.ANY)
+    vmem_spec = pl.BlockSpec(memory_space=pltpu.VMEM)
+    return pl.pallas_call(
+        main_kernel,
+        out_shape=jax.ShapeDtypeStruct((BLOCKS, ROWS, WIDTH), bf16),
+        in_specs=[smem_spec, smem_spec, vmem_spec, any_spec, any_spec],
+        out_specs=vmem_spec,
+        scratch_shapes=[
+            vmem((ROOTS, ROWS, BAND), bf16),
+            vmem((ROOTS, ROWS, BAND), bf16),
+            vmem((ROOTS, ROWS, BAND), bf16),
+            vmem((6 * TRAINS, ROWS, BAND), bf16),
+            vmem((2 * STEPS, ROWS, BAND), bf16),
+            vmem((WIDTH, WIDTH), bf16),
+            vmem((HALF, WIDTH), bf16),
+            vmem((HALF, REST), bf16),
+            vmem((HALF, WIDTH), bf16),
+            vmem((HALF, REST), bf16),
+            vmem((HALF, WIDTH), bf16),
+            vmem((HALF, HALF), f32),
+            vmem((HALF, HALF), bf16),
+            vmem((4, 8, TILE), f32),
+            vmem((8, TILE), f32),
+            dma((2, 5)),
+            dma((2, 3, TRAINS)),
+            dma((2, HOPS, TRAINS)),
+            dma((SHARDS,)),
+            dma(()),
+            dma((SHARDS,)),
+            dma((2,)),
+            dma((SHARDS,)),
+            dma((2,)),
+            dma((3,)),
+            dma(()),
+            dma(()),
+            dma((16,)),
+            dma(()),
+        ],
+        compiler_params=pltpu.CompilerParams(
+            collective_id=1, has_side_effects=True, vmem_limit_bytes=48 << 20
+        ),
+    )(table, packed, grad_blocks, stale_roots, fresh_roots)
+
+
+def local(grad_blocks, stale_roots, fresh_roots, owner_list, slot_list, refresh_flags):
+    packed = jnp.where(refresh_flags == 1, owner_list * 32 + slot_list, -1).astype(jnp.int32)
+    table = schedule(packed)
+
+    def by_ring(_):
+        return ring_exchange(table, packed.reshape(-1), grad_blocks, stale_roots, fresh_roots)
+
+    def by_all(_):
+        return whole_exchange(
+            grad_blocks, stale_roots, fresh_roots, owner_list, slot_list, refresh_flags
+        )
+
+    return lax.cond(table[OK_ROW] == 0, by_ring, by_all, None)
+
+
 def solution(mesh):
     placed = (
         P("group", "fsdp", None),

time: 397 us -> 143 us (0.36)
  blocking collectives: 289 us -> 0 us
  Pallas kernels: 0 us -> 137 us
  waiting for transfers between devices: 56.2 us -> 0 us
  starting transfers between devices: 20.5 us -> 0 us
  matrix products: 11.3 us -> 0 us
  local copies, waits for them, and re-layouts: 13.5 us -> 4.57 us
  other arithmetic: 5.98 us -> 0.01 us
    all_to_all x1 -> x0, blocking collectives: 224 us -> none  [local(): lax.all_to_all(outgoing, 'group', split_axis=0, concat_axis=0, tiled=True)]
    pallas_call x0 -> x2, Pallas kernels: none -> 137 us  [the longest x1 133 us: ring_exchange(): pl.pallas_call(main_kernel, out_shape=jax.ShapeDtypeStruct((BLOCKS, ROWS,...]
    psum x1 -> x0, blocking collectives: 64.4 us -> none  [local(): grad_square, update_square = lax.psum((grad_square, update_square), 'fsdp')]
    all_to_all x3 -> x0, waiting for transfers between devices: 56.2 us -> none  [the longest x1 27.6 us: local(): lax.all_to_all(pieces, 'fsdp', split_axis=0, concat_axis=1, tiled=True)]
    all_to_all x3 -> x0, starting transfers between devices: 20.5 us -> none  [the longest x1 8.35 us: local(): lax.all_to_all(jnp.repeat(grad_blocks, spread, axis=0), 'fsdp', split_axi...]
    dot_general x3 -> x0, matrix products: 11.3 us -> none  [the longest x1 5.71 us: local(): jnp.einsum('rt,txw->rxw', chooser, arrived, preferred_element_type=jnp.fl...]
    slice x2, local copies, waits for them, and re-layouts: 7.93 us -> 0.52 us  [the longest x1 0.52 us: local(): return lax.cond(table[OK_ROW] == 0, by_ring, by_all, None)]
  transfers between devices with their start and end apart: 3 -> 0, of which waited for: 3 -> 0; matrix products, arithmetic and copies ran while one was open for 4% -> 0% of each run, Pallas kernels for 0% -> 0%
where the time goes in v1:
time: 143 us; the launch traced here: 142 us
  Pallas kernels  137 us (96%)
  local copies, waits for them, and re-layouts  4.57 us (3%)
    pallas_call x1, Pallas kernels, ring_exchange(): pl.pallas_call(main_kernel, out_shape=jax.ShapeDtypeStruct((BLOCKS, ROWS,...  133 us
    pallas_call x1, Pallas kernels, schedule(): pl.pallas_call(schedule_kernel, out_shape=jax.ShapeDtypeStruct((TABLE_ROW...  3.64 us
    unnamed x4, local copies, waits for them, and re-layouts  3.11 us

profile of v1, /device:TPU:1, one launch (start us, length us, event | category | flops | bytes accessed | tf_op | source)
XLA Modules:
  0.0 142.2 jit_solution(12426838382750160300)
XLA Ops:
  0.0 0.8 copy.46
  0.8 0.8 copy.45
  1.5 0.8 copy.44
  2.3 0.1 copy.47
  2.4 0.7 tile.10.packed_ref
  3.1 3.6 %shard_map.66 = s32[184,128]{1,0:T(8,128)S(1)} custom-call(s32[16,128]{1,0:T(8,128)} %tile.10.packed_ref), custom_call_target="tpu_custom_call" | custom-call | tf_op jit(solution)/shard_map/pallas_call | solution.py:188
  6.7 0.5 slice.38
  7.9 133.5 %conditional.1 = (bf16[8,32,1024]{2,1,0:T(8,128)(2,1)S(1)}) conditional(s32[]{:T(128)} %bitcast.20, (bf16[8,32,1024]{2,1,0:T(8,128)(2,1)}, s32[32,16]{0,1:T(8,128)}, s32[32,16]{0,1:T(8,128)}, s32[32,16]{0,1:T(8,128)}, bf16[16,32,1024]{2,1,0:T(8,128)(2,1)}, /*index=5*/bf16[16,32,1024]{2,1,0:T(8,128)(2,1)}) %tuple.11, (s32[184,128]{1,0:T(8,128)S(1)}, ...), branch_computations={%region_0.7_spmd, %region_7.8_spmd} | conditional | flops 1687163392 | bytes 58741988 | solution.py:571
  8.1 0.1 copy.53
  8.2 0.1 reshape.60.packed
  8.3 132.9 %branch_1_fun.1 = bf16[8,32,1024]{2,1,0:T(8,128)(2,1)S(1)} custom-call(s32[184]{0:T(256)S(1)} %bitcast.35, s32[512]{0:T(512)S(1)} %reshape.60.packed, bf16[8,32,1024]{2,1,0:T(8,128)(2,1)} %get-tuple-element.40.grad, bf16[16,32,1024]{2,1,0:T(8,128)(2,1)} %get-tuple-element.41.stale, bf16[16,32,1024]{2,1,0:T(8,128)(2,1)} %get-tuple-element.42.fresh), custom_call_target="tpu_custom_call" | custom-call | tf_op jit(solution)/shard_map/cond/branch_1_fun/pallas_call | solution.py:517
  141.4 0.8 copy.67
  (3 shorter events, 0.0 us)

commit v2 on v1

--- a/solution.py
+++ b/solution.py
@@ -25,7 +25,8 @@
 TRAINS = 4
 STEPS = HOPS * TRAINS
 DIST_ROWS = 2 * STEPS
-OK_ROW = DIST_ROWS + 2 * REACH
+CODE_ROW = DIST_ROWS + 2 * REACH
+OK_ROW = CODE_ROW + ROOTS
 TABLE_ROWS = OK_ROW + 8
 
 
@@ -114,12 +115,14 @@
     )
 
 
-def schedule_kernel(packed_ref, table_ref, ahead, log):
+def schedule_kernel(owner_ref, slot_ref, flag_ref, table_ref, ahead, log):
     group_pos = lax.axis_index("group")
     lane = lax.broadcasted_iota(jnp.int32, (1, TILE), 1)
     node = lane % GROUPS
     rows = lax.broadcasted_iota(jnp.int32, (REACH, TILE), 0)
-    packed = packed_ref[...]
+    packed = jnp.where(flag_ref[...] == 1, owner_ref[...] * 32 + slot_ref[...], -1)
+    packed = jnp.concatenate([packed] * (TILE // GROUPS), axis=1)
+    log[CODE_ROW:OK_ROW, :] = packed
     owner = jnp.where(packed < 0, -1, packed // 32)
     value = jnp.where(packed < 0, 0, packed % 32 + 1)
     for dist in range(1, GROUPS):
@@ -173,7 +176,7 @@
     )
     waiting, arrived, remain, _ = lax.fori_loop(0, HOPS, hop, start)
     log[DIST_ROWS : DIST_ROWS + REACH, :] = arrived[0]
-    log[DIST_ROWS + REACH : OK_ROW, :] = arrived[1]
+    log[DIST_ROWS + REACH : CODE_ROW, :] = arrived[1]
     open_count = jnp.max(jnp.maximum(waiting[0], waiting[1]), axis=0, keepdims=True)
     for count in remain:
         open_count = jnp.maximum(open_count, count)
@@ -183,18 +186,17 @@
     table_ref[...] = jnp.broadcast_to(own, (TABLE_ROWS, TILE))
 
 
-def schedule(packed):
-    lanes = jnp.tile(packed.T, (1, TILE // GROUPS))
+def schedule(owner_list, slot_list, refresh_flags):
     table = pl.pallas_call(
         schedule_kernel,
         out_shape=jax.ShapeDtypeStruct((TABLE_ROWS, TILE), jnp.int32),
-        in_specs=[pl.BlockSpec(memory_space=pltpu.VMEM)],
+        in_specs=[pl.BlockSpec(memory_space=pltpu.VMEM)] * 3,
         out_specs=pl.BlockSpec(memory_space=pltpu.VMEM),
         scratch_shapes=[
             pltpu.VMEM((2, REACH, TILE), jnp.int32),
             pltpu.VMEM((TABLE_ROWS, TILE), jnp.int32),
         ],
-    )(lanes)
+    )(owner_list.T, slot_list.T, refresh_flags.T)
     return table[:, 0]
 
 
@@ -202,12 +204,16 @@
     return tile.astype(jnp.float32).T.astype(jnp.bfloat16)
 
 
-def fill(inner, outer):
+def fill_near(inner):
     for row in range(4):
         for col in range(row):
             inner[row * TILE : (row + 1) * TILE, col * TILE : (col + 1) * TILE] = turned(
                 inner[col * TILE : (col + 1) * TILE, row * TILE : (row + 1) * TILE]
             )
+
+
+def fill_far(inner, outer):
+    for row in range(4):
         for col in range(row + 5, SUPER):
             away = row + SUPER - col - 1
             inner[row * TILE : (row + 1) * TILE, col * TILE : (col + 1) * TILE] = turned(
@@ -216,17 +222,20 @@
 
 
 def main_kernel(
-    table, packed, grad, stale, fresh, out,
+    table, grad, stale, fresh, out,
     fresh_band, stale_band, current, sending, log, whole_grad,
-    left_in, left_out, right_in, right_out, left_product, product, tile, sums, sums_out,
-    load_sem, ring_send, ring_recv, grad_send, grad_recv, left_send, left_recv,
-    right_send, right_recv, sum_send, sum_recv, own_sem, tile_send, tile_recv,
+    left_in, left_out, right_in, right_out, left_product, product, tile, tiles, sums, sums_out,
+    load_sem, ring_send, ring_recv, grad_send, grad_recv, left_send, left_recv, left_pass,
+    left_passed, right_send, right_recv, right_pass, right_passed, sum_send, sum_recv,
+    tile_send, tile_recv,
 ):
     z = lax.axis_index("group")
     f = lax.axis_index("fsdp")
     onward = (lax.rem(z + 1, GROUPS), lax.rem(z + GROUPS - 1, GROUPS))
     superblock = f // 4
     block = f // 4
+    place = lax.rem(f, 16)
+    own_half = f // 16
     part = lax.rem(f, 4)
     row_half = part // 2
     col_half = lax.rem(part, 2)
@@ -324,8 +333,8 @@
             for turn in range(3):
                 ring_copy(way, HOPS - 3 + turn, train).wait_send()
 
-    for root in range(ROOTS):
-        code = packed[z * ROOTS + root]
+    def choose(root):
+        code = table[CODE_ROW + root]
         used = jnp.maximum(code, 0)
         owner = used // 32
         slot = lax.rem(used, 32)
@@ -338,33 +347,14 @@
         own = jnp.where(away == 0, fresh_band[slot], moved)
         current[root] = jnp.where(code < 0, stale_band[root], own)
 
-    def root_copies(number, half, peer_half, peer, inner, outer, send, recv, recv_out):
-        place = lax.rem(f + SHARDS - 16 * peer_half, SHARDS)
-        first_row = pl.multiple_of(lax.rem(place, 16) * ROWS, ROWS)
-        col = pl.multiple_of(lax.rem(place // 4, 4) * TILE, TILE)
-        near = (
-            current.at[number],
-            inner.at[pl.ds(first_row, ROWS), pl.ds(col, BAND)],
-        )
-        far = (
-            current.at[number, :, pl.ds(TILE, REST)],
-            outer.at[pl.ds(first_row, ROWS), :],
-        )
-        return place < 16, near, far
-
-    def root_send(side, peer, wait):
-        part = lax.rem(peer, 4)
-        half = part // 2 if side == 0 else lax.rem(part, 2)
-        number = (peer // 4) * 2 + side
-        inner, outer, send, recv = (
-            (left_in, left_out, left_send, left_recv),
-            (right_in, right_out, right_send, right_recv),
-        )[side]
-        is_near, near, far = root_copies(number, 0, half, peer, inner, outer, send, recv, recv)
-
-        def go(pair, sem):
+    own_rows = pl.ds(pl.multiple_of(place * ROWS, ROWS), ROWS)
+    own_band = pl.ds(pl.multiple_of((place // 4) * TILE, TILE), BAND)
+
+    def deliver(source, target, peer, send_sem, recv_sem, wait):
+        @pl.when(peer != f)
+        def _():
             copy = pltpu.make_async_remote_copy(
-                src_ref=pair[0], dst_ref=pair[1], send_sem=send.at[peer], recv_sem=sem,
+                src_ref=source, dst_ref=target, send_sem=send_sem, recv_sem=recv_sem,
                 device_id=(z, peer), device_id_type=MESH,
             )
             if wait:
@@ -372,142 +362,158 @@
             else:
                 copy.start()
 
-        @pl.when(is_near)
+        if not wait:
+
+            @pl.when(peer == f)
+            def _():
+                pltpu.make_async_copy(source, target, recv_sem).start()
+
+    def left_send_step(step, wait):
+        turn = lax.rem(f + step, 16)
+        number = turn // 2
+        half = lax.rem(turn, 2)
+        peer = 4 * number + 2 * half + place // 8
+        root = current.at[2 * number]
+
+        @pl.when(half == own_half)
         def _():
-            go(near, recv.at[0])
-
-        @pl.when(jnp.logical_not(is_near))
+            deliver(root, left_in.at[own_rows, own_band], peer, left_send.at[turn], left_recv.at[0], wait)
+
+        @pl.when(half != own_half)
         def _():
-            go(far, recv.at[1])
-
-    def root_own(side):
-        part = lax.rem(f, 4)
-        half = part // 2 if side == 0 else lax.rem(part, 2)
-        number = (f // 4) * 2 + side
-        inner, outer, recv = ((left_in, left_out, left_recv), (right_in, right_out, right_recv))[side]
-        is_near, near, far = root_copies(number, 0, half, f, inner, outer, None, None, None)
-
-        @pl.when(is_near)
-        def _():
-            pltpu.make_async_copy(*near, recv.at[0]).start()
-
-        @pl.when(jnp.logical_not(is_near))
-        def _():
-            pltpu.make_async_copy(*far, recv.at[1]).start()
-
-    def root_wait(side):
-        inner, outer, recv = ((left_in, left_out, left_recv), (right_in, right_out, right_recv))[side]
-        window = inner.at[:, pl.ds(0, BAND)]
-        pltpu.make_async_copy(window, window, recv.at[0]).wait()
-        pltpu.make_async_copy(outer, outer, recv.at[1]).wait()
-
-    for side in range(2):
-        each_peer(functools.partial(root_send, side, wait=False))
-        root_own(side)
-
-    root_wait(0)
-    fill(left_in, left_out)
-    first_rows = pl.ds(0, HALF)
-
-    def left_step(index, carry):
+            deliver(
+                root.at[:, pl.ds(TILE, REST)], left_out.at[own_rows, :], peer,
+                left_send.at[turn], left_recv.at[1], wait,
+            )
+
+    def right_send_step(step, wait):
+        turn = lax.rem(f + step, 16)
+        number = turn // 2
+        peer = 4 * number + 2 * lax.rem(turn, 2) + own_half
+        root = current.at[2 * number + 1]
+        deliver(root, right_in.at[own_rows, own_band], peer, right_send.at[turn], right_recv, wait)
+
+    def repeat(count, act):
+        lax.fori_loop(0, count, lambda i, c: (act(i), c)[1], 0)
+
+    for root in range(0, ROOTS, 2):
+        choose(root)
+    repeat(16, lambda step: left_send_step(step, False))
+    for root in range(1, ROOTS, 2):
+        choose(root)
+    repeat(16, lambda step: right_send_step(step, False))
+
+    sibling = f + 1 - 2 * col_half
+
+    def hand(source, target, send_sem, recv_sem):
+        return pltpu.make_async_remote_copy(
+            src_ref=source, dst_ref=target, send_sem=send_sem, recv_sem=recv_sem,
+            device_id=(z, sibling), device_id_type=MESH,
+        )
+
+    def await_bytes(window, sem):
+        pltpu.make_async_copy(window, window, sem).wait()
+
+    await_bytes(left_in.at[pl.ds(0, 256), pl.ds(0, BAND)], left_recv.at[0])
+    await_bytes(left_out.at[pl.ds(0, 256), :], left_recv.at[1])
+    hands = []
+    for index in range(2):
+        start = pl.multiple_of((2 * col_half + index) * TILE, TILE)
+        window = left_in.at[pl.ds(start, TILE), pl.ds(start, BAND)]
+        hands.append(hand(window, window, left_pass.at[index], left_passed))
+    window = left_out.at[pl.ds(pl.multiple_of(256 * col_half, 256), 256), :]
+    hands.append(hand(window, window, left_pass.at[2], left_passed))
+    for copy in hands:
+        copy.start()
+    await_bytes(left_in.at[pl.ds(0, 256), :], left_passed)
+
+    fill_near(left_in)
+    fill_far(left_in, left_out)
+
+    def left_step(index):
         cols = pl.ds(pl.multiple_of(index * 256, 256), 256)
         left_product[:, cols] = jnp.dot(
             left_in[...], whole_grad[:, cols], preferred_element_type=jnp.float32
         ).astype(jnp.bfloat16)
-        return carry
-
-    lax.fori_loop(0, 4, left_step, 0)
-    root_wait(1)
-    fill(right_in, right_out)
+
+    repeat(4, left_step)
+
+    await_bytes(right_in.at[:, pl.ds(0, BAND)], right_recv)
+    for index in range(4):
+        rows = pl.ds(index * TILE, TILE)
+        source = right_in.at[rows, pl.ds((index + 1) * TILE, REST)]
+        copy = hand(source, right_out.at[rows, :], right_pass.at[index], right_passed)
+        copy.start()
+        hands.append(copy)
+    fill_near(right_in)
     near_cols = pl.ds(pl.multiple_of(col_half * HALF, HALF), HALF)
-    far_cols = pl.ds(pl.multiple_of((1 - col_half) * HALF, HALF), HALF)
-    contract_last = (((1,), (1,)), ((), ()))
-
-    def right_step(index, total):
+    next_cols = pl.ds(pl.multiple_of((1 - col_half) * HALF, HALF), TILE)
+    last_cols = pl.ds(pl.multiple_of((1 - col_half) * HALF + TILE, TILE), REST)
+
+    def times(rows, cols, start, size):
+        return lax.dot_general(
+            left_product[rows, cols], right_in[:, start : start + size], (((1,), (1,)), ((), ())),
+            preferred_element_type=jnp.float32,
+        )
+
+    def near_step(index):
         rows = pl.ds(pl.multiple_of(index * TILE, TILE), TILE)
-        value = lax.dot_general(
-            left_product[rows, near_cols], right_in[:, :HALF], contract_last,
-            preferred_element_type=jnp.float32,
-        ) + lax.dot_general(
-            left_product[rows, far_cols], right_in[:, HALF:], contract_last,
-            preferred_element_type=jnp.float32,
-        )
-        product[rows, :] = value
+        product[rows, :] = times(rows, near_cols, 0, HALF) + times(rows, next_cols, HALF, TILE)
+
+    repeat(4, near_step)
+    await_bytes(right_out, right_passed)
+    fill_far(right_in, right_out)
+
+    def tile_step(chunk, index, wait):
+        row = chunk * 4 + index
+        deliver(
+            tile.at[pl.ds(pl.multiple_of(row * ROWS, ROWS), ROWS), :],
+            tiles.at[block, :, near_cols],
+            row_half * 16 + row, tile_send.at[row], tile_recv, wait,
+        )
+
+    def last_step(index, total):
+        chunk = lax.rem(index + block, 4)
+        rows = pl.ds(pl.multiple_of(chunk * TILE, TILE), TILE)
+        value = product[rows, :] + times(rows, last_cols, BAND, REST)
+        tile[rows, :] = value.astype(jnp.bfloat16)
+        repeat(4, lambda turn: tile_step(chunk, turn, False))
         squares = (value * value).reshape(16, 8, 4, TILE)
         return total + jnp.sum(squares, axis=(0, 2))
 
-    own_square = lax.fori_loop(0, 4, right_step, jnp.zeros((8, TILE), jnp.float32))
-    sums_out[...] = own_square
-
-    def sum_copy(step):
-        peer = (f // 4) * 4 + lax.rem(part + step, 4)
-        return pltpu.make_async_remote_copy(
-            src_ref=sums_out, dst_ref=sums.at[part], send_sem=sum_send.at[step - 1],
-            recv_sem=sum_recv, device_id=(z, peer), device_id_type=MESH,
-        )
-
-    for step in range(1, 4):
-        sum_copy(step).start()
-    pltpu.make_async_copy(sums_out, sums.at[part], sum_recv).start()
-    pltpu.make_async_copy(sums, sums, sum_recv).wait()
-    update_square = (sums[0] + sums[1]) + (sums[2] + sums[3])
-    update_square = jnp.sum(update_square, axis=(0, 1), keepdims=True)
-    grad_total = jnp.sum(grad_square, axis=(0, 1), keepdims=True)
-    ratio = jnp.sqrt(grad_total) * lax.rsqrt(update_square + epsilon)
-
-    def scale_step(index, carry):
-        rows = pl.ds(pl.multiple_of(index * 64, 64), 64)
-        tile[rows, :] = (ratio * product[rows, :]).astype(jnp.bfloat16)
-        return carry
-
-    lax.fori_loop(0, 8, scale_step, 0)
-
-    def tile_copy(step):
-        row = pl.multiple_of(step * ROWS, ROWS)
-        return (
-            tile.at[pl.ds(row, ROWS), :],
-            out.at[block, :, pl.ds(pl.multiple_of(col_half * HALF, HALF), HALF)],
-        )
-
-    def tile_remote(step):
-        source, target = tile_copy(step)
-        return pltpu.make_async_remote_copy(
-            src_ref=source, dst_ref=target, send_sem=tile_send.at[step], recv_sem=tile_recv,
-            device_id=(z, row_half * 16 + step), device_id_type=MESH,
-        )
-
-    def tile_act(wait):
-        def act(step, carry):
-            turn = lax.rem(f + step, 16)
-
-            @pl.when(row_half * 16 + turn != f)
-            def _():
-                copy = tile_remote(turn)
-                if wait:
-                    copy.wait_send()
-                else:
-                    copy.start()
-
-            return carry
-
-        lax.fori_loop(0, 16, act, 0)
-
-    tile_act(False)
-
-    @pl.when(row_half == f // 16)
-    def _():
-        pltpu.make_async_copy(*tile_copy(lax.rem(f, 16)), tile_recv).start()
+    update_part = lax.fori_loop(0, 4, last_step, jnp.zeros((8, TILE), jnp.float32))
+    update_part = jnp.sum(update_part, axis=0, keepdims=True)
+    grad_part = jnp.sum(grad_square, axis=0, keepdims=True)
+    line = lax.broadcasted_iota(jnp.int32, (8, TILE), 0)
+    sums_out[...] = jnp.where(line == 0, update_part, grad_part)
+
+    def sum_step(step, wait):
+        peer = lax.rem(f + step, SHARDS)
+        deliver(sums_out, sums.at[f], peer, sum_send.at[step], sum_recv, wait)
+
+    repeat(SHARDS, lambda step: sum_step(step, False))
 
     each_peer(lambda peer: grad_remote(peer).wait_send())
-    for side in range(2):
-        each_peer(functools.partial(root_send, side, wait=True))
-    for step in range(1, 4):
-        sum_copy(step).wait_send()
-    tile_act(True)
-    pltpu.make_async_copy(out, out, tile_recv).wait()
-
-
-def ring_exchange(table, packed, grad_blocks, stale_roots, fresh_roots):
+    repeat(16, lambda step: left_send_step(step, True))
+    repeat(16, lambda step: right_send_step(step, True))
+    for copy in hands:
+        copy.wait_send()
+    await_bytes(sums, sum_recv)
+    ratios = []
+    for number in range(BLOCKS):
+        parts = [sums[4 * number + index] for index in range(4)]
+        update_square = (parts[0] + parts[1]) + (parts[2] + parts[3])
+        update_square = jnp.sum(update_square[0:1, :], axis=1, keepdims=True)
+        grad_total = jnp.sum(parts[0][1:2, :], axis=1, keepdims=True)
+        ratios.append(jnp.sqrt(grad_total) * lax.rsqrt(update_square + epsilon))
+    await_bytes(tiles, tile_recv)
+    for number in range(BLOCKS):
+        out[number] = (ratios[number] * tiles[number].astype(jnp.float32)).astype(jnp.bfloat16)
+    repeat(16, lambda row: tile_step(row // 4, lax.rem(row, 4), True))
+    repeat(SHARDS, lambda step: sum_step(step, True))
+
+
+def ring_exchange(table, grad_blocks, stale_roots, fresh_roots):
     bf16, f32 = jnp.bfloat16, jnp.float32
     dma = pltpu.SemaphoreType.DMA
     vmem = pltpu.VMEM
@@ -517,7 +523,7 @@
     return pl.pallas_call(
         main_kernel,
         out_shape=jax.ShapeDtypeStruct((BLOCKS, ROWS, WIDTH), bf16),
-        in_specs=[smem_spec, smem_spec, vmem_spec, any_spec, any_spec],
+        in_specs=[smem_spec, vmem_spec, any_spec, any_spec],
         out_specs=vmem_spec,
         scratch_shapes=[
             vmem((ROOTS, ROWS, BAND), bf16),
@@ -533,19 +539,23 @@
             vmem((HALF, WIDTH), bf16),
             vmem((HALF, HALF), f32),
             vmem((HALF, HALF), bf16),
-            vmem((4, 8, TILE), f32),
+            vmem((BLOCKS, ROWS, WIDTH), bf16),
+            vmem((SHARDS, 8, TILE), f32),
             vmem((8, TILE), f32),
             dma((2, 5)),
             dma((2, 3, TRAINS)),
             dma((2, HOPS, TRAINS)),
             dma((SHARDS,)),
             dma(()),
-            dma((SHARDS,)),
-            dma((2,)),
-            dma((SHARDS,)),
+            dma((16,)),
             dma((2,)),
             dma((3,)),
             dma(()),
+            dma((16,)),
+            dma(()),
+            dma((4,)),
+            dma(()),
+            dma((SHARDS,)),
             dma(()),
             dma((16,)),
             dma(()),
@@ -553,15 +563,14 @@
         compiler_params=pltpu.CompilerParams(
             collective_id=1, has_side_effects=True, vmem_limit_bytes=48 << 20
         ),
-    )(table, packed, grad_blocks, stale_roots, fresh_roots)
+    )(table, grad_blocks, stale_roots, fresh_roots)
 
 
 def local(grad_blocks, stale_roots, fresh_roots, owner_list, slot_list, refresh_flags):
-    packed = jnp.where(refresh_flags == 1, owner_list * 32 + slot_list, -1).astype(jnp.int32)
-    table = schedule(packed)
+    table = schedule(owner_list, slot_list, refresh_flags)
 
     def by_ring(_):
-        return ring_exchange(table, packed.reshape(-1), grad_blocks, stale_roots, fresh_roots)
+        return ring_exchange(table, grad_blocks, stale_roots, fresh_roots)
 
     def by_all(_):
         return whole_exchange(

time: 143 us -> 128 us (0.90)
  Pallas kernels: 137 us -> 126 us
  local copies, waits for them, and re-layouts: 4.57 us -> 1.41 us
    pallas_call x1, Pallas kernels: 133 us -> 122 us  [ring_exchange(): pl.pallas_call(main_kernel, out_shape=jax.ShapeDtypeStruct((BLOCKS, ROWS,...]
    unnamed x4 -> x1, local copies, waits for them, and re-layouts: 3.11 us -> 0.8 us
where the time goes in v2:
time: 128 us
  Pallas kernels  126 us (98%)
  local copies, waits for them, and re-layouts  1.41 us (1%)
    pallas_call x1, Pallas kernels, ring_exchange(): pl.pallas_call(main_kernel, out_shape=jax.ShapeDtypeStruct((BLOCKS, ROWS,...  122 us
    pallas_call x1, Pallas kernels, schedule(): pl.pallas_call(schedule_kernel, out_shape=jax.ShapeDtypeStruct((TABLE_ROW...  3.75 us

profile of v2, /device:TPU:1, one launch (start us, length us, event | category | flops | bytes accessed | tf_op | source)
XLA Modules:
  0.0 128.1 jit_solution(13110066390468462239)
XLA Ops:
  0.0 3.7 %shard_map.66 = s32[200,128]{1,0:T(8,128)S(1)} custom-call(s32[16,32]{1,0:T(8,128)} %bitcast.44, s32[16,32]{1,0:T(8,128)} %bitcast.45, s32[16,32]{1,0:T(8,128)} %bitcast.46), custom_call_target="tpu_custom_call" | custom-call | tf_op jit(solution)/shard_map/pallas_call | solution.py:190
  3.7 0.5 slice.38
  4.9 122.3 %conditional.1 = (bf16[8,32,1024]{2,1,0:T(8,128)(2,1)S(1)}) conditional(s32[]{:T(128)} %bitcast.22, (bf16[8,32,1024]{2,1,0:T(8,128)(2,1)}, s32[32,16]{0,1:T(8,128)}, s32[32,16]{0,1:T(8,128)}, s32[32,16]{0,1:T(8,128)}, bf16[16,32,1024]{2,1,0:T(8,128)(2,1)}, /*index=5*/bf16[16,32,1024]{2,1,0:T(8,128)(2,1)}) %tuple.11, (s32[200,128]{1,0:T(8,128)S(1)}, ...), branch_computations={%region_0.7_spmd, %region_7.8_spmd} | conditional | flops 1687163392 | bytes 58741988 | solution.py:580
  5.1 0.1 copy.41
  5.2 122.0 %branch_1_fun.1 = bf16[8,32,1024]{2,1,0:T(8,128)(2,1)S(1)} custom-call(s32[200]{0:T(256)S(1)} %bitcast.37, bf16[8,32,1024]{2,1,0:T(8,128)(2,1)} %get-tuple-element.37.grad, bf16[16,32,1024]{2,1,0:T(8,128)(2,1)} %get-tuple-element.38.stale, bf16[16,32,1024]{2,1,0:T(8,128)(2,1)} %get-tuple-element.39.fresh), custom_call_target="tpu_custom_call" | custom-call | tf_op jit(solution)/shard_map/cond/branch_1_fun/pallas_call | solution.py:523
  127.3 0.8 copy.55
  (1 shorter events, 0.0 us)

commit v3 on v2

--- a/solution.py
+++ b/solution.py
@@ -21,13 +21,15 @@
 BAND = 640
 REST = 384
 REACH = 16
-HOPS = 18
+HOPS = (16, 20)
+MOST = HOPS[-1]
+GRADS_A_HOP = 3
 TRAINS = 4
-STEPS = HOPS * TRAINS
+STEPS = MOST * TRAINS
 DIST_ROWS = 2 * STEPS
 CODE_ROW = DIST_ROWS + 2 * REACH
-OK_ROW = CODE_ROW + ROOTS
-TABLE_ROWS = OK_ROW + 8
+NEED_ROW = CODE_ROW + ROOTS
+TABLE_ROWS = NEED_ROW + 8
 
 
 def tile_return(
@@ -122,13 +124,12 @@
     rows = lax.broadcasted_iota(jnp.int32, (REACH, TILE), 0)
     packed = jnp.where(flag_ref[...] == 1, owner_ref[...] * 32 + slot_ref[...], -1)
     packed = jnp.concatenate([packed] * (TILE // GROUPS), axis=1)
-    log[CODE_ROW:OK_ROW, :] = packed
-    owner = jnp.where(packed < 0, -1, packed // 32)
-    value = jnp.where(packed < 0, 0, packed % 32 + 1)
+    log[CODE_ROW:NEED_ROW, :] = packed
     for dist in range(1, GROUPS):
-        shift = (TILE - dist) % TILE
-        match = pltpu.roll(owner, shift, 1) == node
-        line = jnp.max(jnp.where(match, pltpu.roll(value, shift, 1), 0), axis=0, keepdims=True)
+        seen = pltpu.roll(packed, (TILE - dist) % TILE, 1)
+        match = jnp.right_shift(seen, 5) == node
+        line = jnp.where(match, jnp.bitwise_and(seen, 31) + 1, 0)
+        line = jnp.max(line, axis=0, keepdims=True)
         if dist <= REACH:
             near = jnp.where(line > 0, line + dist * 32, 0)
             if dist == REACH:
@@ -174,14 +175,17 @@
         (zero,) * (2 * TRAINS),
         (zero,) * (2 * TRAINS),
     )
-    waiting, arrived, remain, _ = lax.fori_loop(0, HOPS, hop, start)
+    waiting, arrived, remain, _ = lax.fori_loop(0, MOST, hop, start)
     log[DIST_ROWS : DIST_ROWS + REACH, :] = arrived[0]
     log[DIST_ROWS + REACH : CODE_ROW, :] = arrived[1]
     open_count = jnp.max(jnp.maximum(waiting[0], waiting[1]), axis=0, keepdims=True)
     for count in remain:
         open_count = jnp.maximum(open_count, count)
     open_count = jnp.max(open_count, axis=1, keepdims=True)
-    log[OK_ROW:TABLE_ROWS, :] = jnp.broadcast_to(open_count, (8, TILE))
+    last = jnp.max(jnp.maximum(arrived[0], arrived[1]), axis=0, keepdims=True)
+    need = jnp.max(last, axis=1, keepdims=True) // TRAINS + 1
+    need = jnp.where(open_count > 0, MOST + 1, need)
+    log[NEED_ROW:TABLE_ROWS, :] = jnp.broadcast_to(need, (8, TILE))
     own = jnp.sum(jnp.where(lane == group_pos, log[...], 0), axis=1, keepdims=True)
     table_ref[...] = jnp.broadcast_to(own, (TABLE_ROWS, TILE))
 
@@ -222,12 +226,13 @@
 
 
 def main_kernel(
-    table, grad, stale, fresh, out,
+    hops, table, grad, stale, fresh, out,
     fresh_band, stale_band, current, sending, log, whole_grad,
     left_in, left_out, right_in, right_out, left_product, product, tile, tiles, sums, sums_out,
+    totals, totals_out,
     load_sem, ring_send, ring_recv, grad_send, grad_recv, left_send, left_recv, left_pass,
     left_passed, right_send, right_recv, right_pass, right_passed, sum_send, sum_recv,
-    tile_send, tile_recv,
+    total_send, total_recv, tile_send, tile_recv,
 ):
     z = lax.axis_index("group")
     f = lax.axis_index("fsdp")
@@ -280,6 +285,11 @@
             device_id=(z, peer), device_id_type=MESH,
         )
 
+    def grad_step(index):
+        @pl.when(index < SHARDS)
+        def _():
+            grad_remote(lax.rem(f + index, SHARDS)).start()
+
     def each_peer(act):
         lax.fori_loop(1, SHARDS, lambda s, c: (act(lax.rem(f + s, SHARDS)), c)[1], 0)
 
@@ -313,25 +323,22 @@
                 ring_copy(way, index, train).start()
 
     hop(0, True)
-    each_peer(lambda peer: grad_remote(peer).start())
     own_grad = pltpu.make_async_copy(*grad_copy(f), grad_recv)
     own_grad.start()
-    lax.fori_loop(1, HOPS, lambda i, c: (hop(i, False), c)[1], 0)
-
-    pltpu.make_async_copy(whole_grad, whole_grad, grad_recv).wait()
-
-    def add_squares(index, total):
-        rows = whole_grad[pl.ds(pl.multiple_of(index * 32, 32), 32), :].astype(jnp.float32)
-        squares = (rows * rows).reshape(4, 8, 8, TILE)
-        return total + jnp.sum(squares, axis=(0, 2))
-
-    grad_square = lax.fori_loop(0, WIDTH // 32, add_squares, jnp.zeros((8, TILE), jnp.float32))
+
+    def hop_and_grads(index, carry):
+        hop(index, False)
+        for extra in range(GRADS_A_HOP):
+            grad_step((index - 1) * GRADS_A_HOP + 1 + extra)
+        return carry
+
+    lax.fori_loop(1, hops, hop_and_grads, 0)
 
     for way in range(2):
         for train in range(TRAINS):
-            ring_copy(way, HOPS - 1, train).wait_recv()
+            ring_copy(way, hops - 1, train).wait_recv()
             for turn in range(3):
-                ring_copy(way, HOPS - 3 + turn, train).wait_send()
+                ring_copy(way, hops - 3 + turn, train).wait_send()
 
     def choose(root):
         code = table[CODE_ROW + root]
@@ -414,6 +421,15 @@
     def await_bytes(window, sem):
         pltpu.make_async_copy(window, window, sem).wait()
 
+    pltpu.make_async_copy(whole_grad, whole_grad, grad_recv).wait()
+
+    def add_squares(index, total):
+        rows = whole_grad[pl.ds(pl.multiple_of(index * 32, 32), 32), :].astype(jnp.float32)
+        squares = (rows * rows).reshape(4, 8, 8, TILE)
+        return total + jnp.sum(squares, axis=(0, 2))
+
+    grad_square = lax.fori_loop(0, WIDTH // 32, add_squares, jnp.zeros((8, TILE), jnp.float32))
+
     await_bytes(left_in.at[pl.ds(0, 256), pl.ds(0, BAND)], left_recv.at[0])
     await_bytes(left_out.at[pl.ds(0, 256), :], left_recv.at[1])
     hands = []
@@ -464,8 +480,7 @@
     await_bytes(right_out, right_passed)
     fill_far(right_in, right_out)
 
-    def tile_step(chunk, index, wait):
-        row = chunk * 4 + index
+    def tile_step(row, wait):
         deliver(
             tile.at[pl.ds(pl.multiple_of(row * ROWS, ROWS), ROWS), :],
             tiles.at[block, :, near_cols],
@@ -473,11 +488,9 @@
         )
 
     def last_step(index, total):
-        chunk = lax.rem(index + block, 4)
-        rows = pl.ds(pl.multiple_of(chunk * TILE, TILE), TILE)
+        rows = pl.ds(pl.multiple_of(index * TILE, TILE), TILE)
         value = product[rows, :] + times(rows, last_cols, BAND, REST)
         tile[rows, :] = value.astype(jnp.bfloat16)
-        repeat(4, lambda turn: tile_step(chunk, turn, False))
         squares = (value * value).reshape(16, 8, 4, TILE)
         return total + jnp.sum(squares, axis=(0, 2))
 
@@ -488,32 +501,40 @@
     sums_out[...] = jnp.where(line == 0, update_part, grad_part)
 
     def sum_step(step, wait):
-        peer = lax.rem(f + step, SHARDS)
-        deliver(sums_out, sums.at[f], peer, sum_send.at[step], sum_recv, wait)
-
-    repeat(SHARDS, lambda step: sum_step(step, False))
+        peer = 4 * block + lax.rem(part + step, 4)
+        deliver(sums_out, sums.at[part], peer, sum_send.at[step], sum_recv, wait)
+
+    def total_step(step, wait):
+        peer = row_half * 16 + 2 * lax.rem(step + block, 8) + col_half
+        deliver(totals_out, totals.at[block], peer, total_send.at[step], total_recv, wait)
+
+    repeat(4, lambda step: sum_step(step, False))
+    repeat(16, lambda step: tile_step(lax.rem(step + 4 * block, 16), False))
+    await_bytes(sums, sum_recv)
+    update_part = (sums[0] + sums[1]) + (sums[2] + sums[3])
+    totals_out[...] = jnp.where(line == 0, update_part, grad_part)
+    repeat(8, lambda step: total_step(step, False))
 
     each_peer(lambda peer: grad_remote(peer).wait_send())
     repeat(16, lambda step: left_send_step(step, True))
     repeat(16, lambda step: right_send_step(step, True))
     for copy in hands:
         copy.wait_send()
-    await_bytes(sums, sum_recv)
+    await_bytes(totals, total_recv)
     ratios = []
     for number in range(BLOCKS):
-        parts = [sums[4 * number + index] for index in range(4)]
-        update_square = (parts[0] + parts[1]) + (parts[2] + parts[3])
-        update_square = jnp.sum(update_square[0:1, :], axis=1, keepdims=True)
-        grad_total = jnp.sum(parts[0][1:2, :], axis=1, keepdims=True)
+        update_square = jnp.sum(totals[number, 0:1, :], axis=1, keepdims=True)
+        grad_total = jnp.sum(totals[number, 1:2, :], axis=1, keepdims=True)
         ratios.append(jnp.sqrt(grad_total) * lax.rsqrt(update_square + epsilon))
     await_bytes(tiles, tile_recv)
     for number in range(BLOCKS):
         out[number] = (ratios[number] * tiles[number].astype(jnp.float32)).astype(jnp.bfloat16)
-    repeat(16, lambda row: tile_step(row // 4, lax.rem(row, 4), True))
-    repeat(SHARDS, lambda step: sum_step(step, True))
-
-
-def ring_exchange(table, grad_blocks, stale_roots, fresh_roots):
+    repeat(16, lambda row: tile_step(row, True))
+    repeat(4, lambda step: sum_step(step, True))
+    repeat(8, lambda step: total_step(step, True))
+
+
+def ring_exchange(hops, table, grad_blocks, stale_roots, fresh_roots):
     bf16, f32 = jnp.bfloat16, jnp.float32
     dma = pltpu.SemaphoreType.DMA
     vmem = pltpu.VMEM
@@ -521,9 +542,9 @@
     any_spec = pl.BlockSpec(memory_space=pl.ANY)
     vmem_spec = pl.BlockSpec(memory_space=pltpu.VMEM)
     return pl.pallas_call(
-        main_kernel,
+        functools.partial(main_kernel, hops),
         out_shape=jax.ShapeDtypeStruct((BLOCKS, ROWS, WIDTH), bf16),
-        in_specs=[smem_spec, vmem_spec, any_spec, any_spec],
+        in_specs=[smem_spec, any_spec, any_spec, any_spec],
         out_specs=vmem_spec,
         scratch_shapes=[
             vmem((ROOTS, ROWS, BAND), bf16),
@@ -540,11 +561,13 @@
             vmem((HALF, HALF), f32),
             vmem((HALF, HALF), bf16),
             vmem((BLOCKS, ROWS, WIDTH), bf16),
-            vmem((SHARDS, 8, TILE), f32),
+            vmem((4, 8, TILE), f32),
+            vmem((8, TILE), f32),
+            vmem((BLOCKS, 8, TILE), f32),
             vmem((8, TILE), f32),
             dma((2, 5)),
             dma((2, 3, TRAINS)),
-            dma((2, HOPS, TRAINS)),
+            dma((2, hops, TRAINS)),
             dma((SHARDS,)),
             dma(()),
             dma((16,)),
@@ -555,13 +578,15 @@
             dma(()),
             dma((4,)),
             dma(()),
-            dma((SHARDS,)),
+            dma((4,)),
+            dma(()),
+            dma((8,)),
             dma(()),
             dma((16,)),
             dma(()),
         ],
         compiler_params=pltpu.CompilerParams(
-            collective_id=1, has_side_effects=True, vmem_limit_bytes=48 << 20
+            collective_id=HOPS.index(hops), has_side_effects=True, vmem_limit_bytes=48 << 20
         ),
     )(table, grad_blocks, stale_roots, fresh_roots)
 
@@ -569,15 +594,17 @@
 def local(grad_blocks, stale_roots, fresh_roots, owner_list, slot_list, refresh_flags):
     table = schedule(owner_list, slot_list, refresh_flags)
 
-    def by_ring(_):
-        return ring_exchange(table, grad_blocks, stale_roots, fresh_roots)
+    def by_ring(hops):
+        return lambda _: ring_exchange(hops, table, grad_blocks, stale_roots, fresh_roots)
 
     def by_all(_):
         return whole_exchange(
             grad_blocks, stale_roots, fresh_roots, owner_list, slot_list, refresh_flags
         )
 
-    return lax.cond(table[OK_ROW] == 0, by_ring, by_all, None)
+    need = table[NEED_ROW]
+    path = sum((need > hops).astype(jnp.int32) for hops in HOPS)
+    return lax.switch(path, [by_ring(hops) for hops in HOPS] + [by_all], None)
 
 
 def solution(mesh):

time: 128 us -> 135 us (1.055)
  Pallas kernels: 126 us -> 132 us
    pallas_call x1, Pallas kernels: 122 us -> 128 us  [ring_exchange(): pl.pallas_call(functools.partial(main_kernel, hops), out_shape=jax.ShapeD...]
where the time goes in v3:
time: 135 us
  Pallas kernels  132 us (98%)
  local copies, waits for them, and re-layouts  1.41 us (1%)
    pallas_call x1, Pallas kernels, ring_exchange(): pl.pallas_call(functools.partial(main_kernel, hops), out_shape=jax.ShapeD...  128 us
    pallas_call x1, Pallas kernels, schedule(): pl.pallas_call(schedule_kernel, out_shape=jax.ShapeDtypeStruct((TABLE_ROW...  3.99 us

profile of v3, /device:TPU:1, one launch (start us, length us, event | category | flops | bytes accessed | tf_op | source)
XLA Modules:
  0.0 134.7 jit_solution(12032792634734854418)
XLA Ops:
  0.0 4.0 %shard_map.67 = s32[216,128]{1,0:T(8,128)S(1)} custom-call(s32[16,32]{1,0:T(8,128)} %bitcast.46, s32[16,32]{1,0:T(8,128)} %bitcast.47, s32[16,32]{1,0:T(8,128)} %bitcast.48), custom_call_target="tpu_custom_call" | custom-call | tf_op jit(solution)/shard_map/pallas_call | solution.py:194
  4.0 0.5 slice.42
  5.8 128.1 %conditional.1 = (bf16[8,32,1024]{2,1,0:T(8,128)(2,1)S(1)}) conditional(s32[]{:T(128)} %bitcast.23, (s32[216,128]{1,0:T(8,128)S(1)}, bf16[8,32,1024]{2,1,0:T(8,128)(2,1)}, bf16[16,32,1024]{2,1,0:T(8,128)(2,1)}, bf16[16,32,1024]{2,1,0:T(8,128)(2,1)}) %tuple.14, (s32[216,128]{1,0:T(8,128)S(1)}, bf16[8,32,1024]{2,1,0:T(8,128)(2,1)}, ...), branch_computations={%region_0.0_spmd, %region_1.0_spmd, %region_2.9_spmd} | conditional | flops 1687163392 | bytes 62936320 | solution.py:607
  5.8 0.1 copy.40
  5.9 127.7 %branch_1_fun.1 = bf16[8,32,1024]{2,1,0:T(8,128)(2,1)S(1)} custom-call(s32[216]{0:T(256)S(1)} %bitcast.39, bf16[8,32,1024]{2,1,0:T(8,128)(2,1)} %get-tuple-element.46.grad, bf16[16,32,1024]{2,1,0:T(8,128)(2,1)} %get-tuple-element.47.stale, bf16[16,32,1024]{2,1,0:T(8,128)(2,1)} %get-tuple-element.48.fresh), custom_call_target="tpu_custom_call" | custom-call | tf_op jit(solution)/shard_map/cond/branch_1_fun/pallas_call | solution.py:544
  133.9 0.8 copy.60
  (1 shorter events, 0.0 us)

commit v4 on v3

--- a/solution.py
+++ b/solution.py
@@ -245,6 +245,17 @@
     row_half = part // 2
     col_half = lax.rem(part, 2)
 
+    barrier = pltpu.get_barrier_semaphore()
+    for peer in onward:
+        pl.semaphore_signal(barrier, inc=1, device_id=(peer, f), device_id_type=MESH)
+
+    def greet(step, carry):
+        peer = lax.rem(f + step, SHARDS)
+        pl.semaphore_signal(barrier, inc=1, device_id=(z, peer), device_id_type=MESH)
+        return carry
+
+    lax.fori_loop(1, SHARDS, greet, 0)
+
     loads = []
     for number, (source, target) in enumerate(((fresh, fresh_band), (stale, stale_band))):
         for col in range(5):
@@ -257,16 +268,6 @@
             load.start()
             loads.append(load)
 
-    barrier = pltpu.get_barrier_semaphore()
-    for peer in onward:
-        pl.semaphore_signal(barrier, inc=1, device_id=(peer, f), device_id_type=MESH)
-
-    def greet(step, carry):
-        peer = lax.rem(f + step, SHARDS)
-        pl.semaphore_signal(barrier, inc=1, device_id=(z, peer), device_id_type=MESH)
-        return carry
-
-    lax.fori_loop(1, SHARDS, greet, 0)
     for load in loads:
         load.wait()
     pl.semaphore_wait(barrier, SHARDS + 1)
@@ -441,18 +442,11 @@
     hands.append(hand(window, window, left_pass.at[2], left_passed))
     for copy in hands:
         copy.start()
-    await_bytes(left_in.at[pl.ds(0, 256), :], left_passed)
-
-    fill_near(left_in)
-    fill_far(left_in, left_out)
-
     def left_step(index):
         cols = pl.ds(pl.multiple_of(index * 256, 256), 256)
         left_product[:, cols] = jnp.dot(
             left_in[...], whole_grad[:, cols], preferred_element_type=jnp.float32
         ).astype(jnp.bfloat16)
-
-    repeat(4, left_step)
 
     await_bytes(right_in.at[:, pl.ds(0, BAND)], right_recv)
     for index in range(4):
@@ -461,6 +455,11 @@
         copy = hand(source, right_out.at[rows, :], right_pass.at[index], right_passed)
         copy.start()
         hands.append(copy)
+    await_bytes(left_in.at[pl.ds(0, 256), :], left_passed)
+
+    fill_near(left_in)
+    fill_far(left_in, left_out)
+    repeat(4, left_step)
     fill_near(right_in)
     near_cols = pl.ds(pl.multiple_of(col_half * HALF, HALF), HALF)
     next_cols = pl.ds(pl.multiple_of((1 - col_half) * HALF, HALF), TILE)

time: 135 us -> 120 us (0.89)
  Pallas kernels: 132 us -> 117 us
    pallas_call x1, Pallas kernels: 128 us -> 113 us  [ring_exchange(): pl.pallas_call(functools.partial(main_kernel, hops), out_shape=jax.ShapeD...]
where the time goes in v4:
time: 120 us
  Pallas kernels  117 us (98%)
  local copies, waits for them, and re-layouts  1.41 us (1%)
  between operations  1.31 us (1%)
    pallas_call x1, Pallas kernels, ring_exchange(): pl.pallas_call(functools.partial(main_kernel, hops), out_shape=jax.ShapeD...  113 us
    pallas_call x1, Pallas kernels, schedule(): pl.pallas_call(schedule_kernel, out_shape=jax.ShapeDtypeStruct((TABLE_ROW...  3.99 us

profile of v4, /device:TPU:1, one launch (start us, length us, event | category | flops | bytes accessed | tf_op | source)
XLA Modules:
  0.0 119.9 jit_solution(15798579192548678878)
XLA Ops:
  0.0 4.0 %shard_map.67 = s32[216,128]{1,0:T(8,128)S(1)} custom-call(s32[16,32]{1,0:T(8,128)} %bitcast.46, s32[16,32]{1,0:T(8,128)} %bitcast.47, s32[16,32]{1,0:T(8,128)} %bitcast.48), custom_call_target="tpu_custom_call" | custom-call | tf_op jit(solution)/shard_map/pallas_call | solution.py:194
  4.0 0.5 slice.42
  5.8 113.3 %conditional.1 = (bf16[8,32,1024]{2,1,0:T(8,128)(2,1)S(1)}) conditional(s32[]{:T(128)} %bitcast.23, (s32[216,128]{1,0:T(8,128)S(1)}, bf16[8,32,1024]{2,1,0:T(8,128)(2,1)}, bf16[16,32,1024]{2,1,0:T(8,128)(2,1)}, bf16[16,32,1024]{2,1,0:T(8,128)(2,1)}) %tuple.14, (s32[216,128]{1,0:T(8,128)S(1)}, bf16[8,32,1024]{2,1,0:T(8,128)(2,1)}, ...), branch_computations={%region_0.0_spmd, %region_1.0_spmd, %region_2.9_spmd} | conditional | flops 1687163392 | bytes 62936320 | solution.py:606
  5.8 0.1 copy.39
  5.9 112.9 %branch_0_fun.1 = bf16[8,32,1024]{2,1,0:T(8,128)(2,1)S(1)} custom-call(s32[216]{0:T(256)S(1)} %bitcast.38, bf16[8,32,1024]{2,1,0:T(8,128)(2,1)} %get-tuple-element.42.grad, bf16[16,32,1024]{2,1,0:T(8,128)(2,1)} %get-tuple-element.43.stale, bf16[16,32,1024]{2,1,0:T(8,128)(2,1)} %get-tuple-element.44.fresh), custom_call_target="tpu_custom_call" | custom-call | tf_op jit(solution)/shard_map/cond/branch_0_fun/pallas_call | solution.py:543
  119.1 0.8 copy.60
  (1 shorter events, 0.0 us)
